TPU v7x, 32 devices: a whole 2x2x4 slice. The times are simulated.
32 devices in a mesh: dp: 2 (over x), expert: 16 (over z, y, core).
Axes of the slice: x: 2, y: 2, z: 4, core: 2. Of those that a mesh axis runs over, the one named last changes fastest.
Arguments:
- tokens: bfloat16 [4096, 1024], P(('dp', 'expert')), may hold values from -6 to 6
- grad_out: bfloat16 [4096, 1024], P(('dp', 'expert')), may hold values from -6 to 6
- expert_ids: int32 [4096, 8], P(('dp', 'expert')), may hold values from 0 to 15, all different within a row; in each aligned block of 128 rows (0 to 127, 128 to 255, ...) at most 72 rows name the same one
- gate_numer: int32 [4096, 8], P(('dp', 'expert')), may hold values from 1 to 16
- w_gate: bfloat16 [16, 1024, 384], P('expert', 'dp'), may hold values from -0.1875 to 0.1875
- w_up: bfloat16 [16, 1024, 384], P('expert', 'dp'), may hold values from -0.1875 to 0.1875
- w_down: bfloat16 [16, 1024, 384], P('expert', 'dp'), may hold values from -0.3125 to 0.3125
Outputs:
- grad_tokens: bfloat16 [4096, 1024], P(('dp', 'expert'))
- grad_gate: bfloat16 [16, 1024, 384], P('expert', 'dp')
- grad_up: bfloat16 [16, 1024, 384], P('expert', 'dp')
- grad_down: bfloat16 [16, 1024, 384], P('expert', 'dp')
Inputs may be any that keep to these rules, and one draw needn't show every extreme that they name: `expert_ids`: each row names 8 different experts. Within the rows of one device no expert is named more than 72 times, and in every draw some expert is named exactly 72 times within some device's rows.
All inputs are finite; a program needn't handle non-finite values.
Results may differ from a plain program's by a relative error of at most 0.0065.
Values may be sent and summed in bfloat16 or wider, within the bound.
A program may use at most 128 MiB of HBM per device.

v0:
```python
import functools

import jax
import jax.numpy as jnp
from jax import lax
from jax.experimental import pallas as pl
from jax.experimental.pallas import tpu as pltpu
from jax.sharding import PartitionSpec as P

MESH = pl.DeviceIdType.MESH
F32 = jnp.float32
BF16 = jnp.bfloat16


def backward_rows(rows_in, grads_in, gate_mat, up_mat, down_mat):
    pre_gate = jnp.dot(rows_in, gate_mat, preferred_element_type=jnp.float32)
    pre_up = jnp.dot(rows_in, up_mat, preferred_element_type=jnp.float32)
    sigmoid_gate = jax.nn.sigmoid(pre_gate)
    activation = (pre_gate * sigmoid_gate * pre_up).astype(jnp.bfloat16)
    grad_act = jnp.dot(grads_in, down_mat, preferred_element_type=jnp.float32)
    grad_up = (grad_act * pre_gate * sigmoid_gate).astype(jnp.bfloat16)
    grad_gate = (grad_act * pre_up * sigmoid_gate * (1.0 + pre_gate * (1.0 - sigmoid_gate))).astype(
        jnp.bfloat16
    )
    grad_rows = jnp.einsum("rf,df->rd", grad_gate, gate_mat, preferred_element_type=jnp.float32)
    grad_rows = grad_rows + jnp.einsum(
        "rf,df->rd", grad_up, up_mat, preferred_element_type=jnp.float32
    )
    return (grad_rows.astype(jnp.bfloat16), grad_gate, grad_up, activation)


def on_device_routed(tokens, grad_out, expert_ids, gate_numer, w_gate, w_up, w_down):
    peers = lax.axis_size("expert")
    data_groups = lax.axis_size("dp")
    tok_rows = tokens.shape[0]
    model_width = tokens.shape[1]
    top_count = expert_ids.shape[1]
    hidden_width = w_gate.shape[2]
    mean_rows = tok_rows * top_count // peers
    capacity = min(tok_rows, mean_rows + tok_rows * top_count // (8 * peers))
    pair_count = tok_rows * top_count
    slot_count = peers * capacity
    numer = gate_numer.astype(jnp.float32)
    gate = numer / jnp.sum(numer, axis=1, keepdims=True)
    scaled = (gate[:, :, None] * grad_out.astype(jnp.float32)[:, None, :]).astype(jnp.bfloat16)
    scaled = scaled.reshape(pair_count, model_width)
    flat_ids = expert_ids.reshape(-1)
    one_hot = (flat_ids[:, None] == jnp.arange(peers, dtype=jnp.int32)[None, :]).astype(
        jnp.bfloat16
    )
    pair_range = jnp.arange(pair_count, dtype=jnp.int32)
    lower = (pair_range[None, :] < pair_range[:, None]).astype(jnp.bfloat16)
    earlier = jnp.dot(lower, one_hot, preferred_element_type=jnp.float32)
    slot = jnp.sum(earlier * one_hot.astype(jnp.float32), axis=1).astype(jnp.int32)
    target = flat_ids * capacity + slot
    pair_of_slot = jnp.full((slot_count,), pair_count, jnp.int32).at[target].set(pair_range)
    token_of_slot = jnp.where(pair_of_slot < pair_count, pair_of_slot // top_count, tok_rows)
    zero_row = jnp.zeros((1, model_width), jnp.bfloat16)
    padded_tokens = jnp.concatenate([tokens, zero_row], axis=0)
    padded_scaled = jnp.concatenate([scaled, zero_row], axis=0)
    send_rows = padded_tokens[token_of_slot].reshape(peers, capacity, model_width)
    send_grads = padded_scaled[pair_of_slot].reshape(peers, capacity, model_width)
    gathered = (
        lax.all_gather(w_gate, "dp", axis=1, tiled=True),
        lax.all_gather(w_up, "dp", axis=1, tiled=True),
        lax.all_gather(w_down, "dp", axis=1, tiled=True),
    )
    gate_mat = gathered[0][0]
    up_mat = gathered[1][0]
    down_mat = gathered[2][0]
    arrived_rows, arrived_grads = (
        lax.all_to_all(send_rows, "expert", split_axis=0, concat_axis=0, tiled=True),
        lax.all_to_all(send_grads, "expert", split_axis=0, concat_axis=0, tiled=True),
    )
    rows_in = arrived_rows.reshape(slot_count, model_width)
    grads_in = arrived_grads.reshape(slot_count, model_width)
    grad_rows, grad_gate, grad_up, activation = backward_rows(
        rows_in, grads_in, gate_mat, up_mat, down_mat
    )
    returned = lax.all_to_all(
        grad_rows.reshape(peers, capacity, model_width),
        "expert",
        split_axis=0,
        concat_axis=0,
        tiled=True,
    )
    picked = returned.reshape(slot_count, model_width)[target].astype(jnp.float32)
    grad_tokens = jnp.sum(picked.reshape(tok_rows, top_count, model_width), axis=1).astype(
        jnp.bfloat16
    )
    quarter = model_width // data_groups
    term_gate = jnp.einsum(
        "rd,rf->df", rows_in, grad_gate, preferred_element_type=jnp.float32
    ).astype(jnp.bfloat16)
    term_up = jnp.einsum("rd,rf->df", rows_in, grad_up, preferred_element_type=jnp.float32).astype(
        jnp.bfloat16
    )
    term_down = jnp.einsum(
        "rd,rf->df", grads_in, activation, preferred_element_type=jnp.float32
    ).astype(jnp.bfloat16)
    stacked = jnp.stack([term_gate, term_up, term_down]).reshape(
        3, data_groups, quarter, hidden_width
    )
    arrived = lax.all_to_all(stacked, "dp", split_axis=1, concat_axis=1, tiled=True)
    summed = jnp.sum(arrived.astype(jnp.float32), axis=1).astype(jnp.bfloat16)
    return (grad_tokens, summed[0][None], summed[1][None], summed[2][None])


def contract_rows(lhs, rhs):
    return lax.dot_general(lhs, rhs, (((0,), (0,)), ((), ())), preferred_element_type=F32)


def layer_kernel(
    chips, tok_ref, grad_ref, ids_ref, numer_ref, wg_ref, wu_ref, wd_ref,
    out_tok, out_gate, out_up, out_down,
    xbuf, gbuf, nbuf, cbuf, sbuf, obuf, rbuf, wgu, wdn, acc_gu, acc_d, pbuf, qbuf, scaled, grads, acts,
    pre_buf, ga_buf, num_ref,
    w_send, w_recv, ring_send, ring_recv, sib_send, sib_recv,
    row_send, row_recv, sum_send, sum_recv, part_send, part_recv,
):
    half_ring = chips // 2
    group = lax.axis_index("dp")
    me = lax.axis_index("expert")
    core = lax.rem(me, 2)
    chip = lax.div(me, 2)
    lane = lax.rem(chip, 2)
    depth = lax.div(chip, 2)
    pos = jnp.where(lane == 0, depth, chips - 1 - depth)

    def device_at(ring_pos):
        far = ring_pos >= half_ring
        along = jnp.where(far, chips - 1 - ring_pos, ring_pos)
        return along * 4 + jnp.where(far, 2, 0) + core

    def ring(offset):
        return lax.rem(pos + offset + chips, chips)

    right = (group, device_at(ring(1)))
    left = (group, device_at(ring(-1)))
    sibling = (group, me + 1 - 2 * core)
    other = (1 - group, me)
    flows = (right, left)

    experts = 2 * chips
    expert_rows = lax.broadcasted_iota(jnp.int32, (experts, ids_ref.shape[1]), 0)
    by_expert = jnp.zeros(expert_rows.shape, jnp.int32)
    total = jnp.zeros(expert_rows.shape, jnp.int32)
    for k in range(ids_ref.shape[0]):
        numer = numer_ref[pl.ds(k, 1), :]
        by_expert = by_expert + jnp.where(ids_ref[pl.ds(k, 1), :] == expert_rows, numer, 0)
        total = total + numer
    num_ref[pl.ds(0, experts), :] = by_expert.astype(F32).astype(BF16)
    num_ref[pl.ds(experts, experts), :] = total.astype(F32).astype(BF16)

    barrier = pltpu.get_barrier_semaphore()
    for target in (right, left, sibling, other):
        pl.semaphore_signal(barrier, inc=1, device_id=target, device_id_type=MESH)
    pl.semaphore_wait(barrier, 4)

    started = []

    def copy(src, dst, send, recv, target):
        return pltpu.make_async_remote_copy(
            src_ref=src, dst_ref=dst, send_sem=send, recv_sem=recv,
            device_id=target, device_id_type=MESH,
        )

    def start(*args):
        op = copy(*args)
        op.start()
        started.append(op)

    share = wg_ref.shape[0]
    hidden = wg_ref.shape[1]
    block, width = tok_ref.shape
    own_at = pl.ds(pl.multiple_of(group * share, share), share)
    other_at = pl.ds(pl.multiple_of((1 - group) * share, share), share)

    def slot(f, d):
        return 0 if d == 0 else min(2 * d - 1 + f, chips - 1)

    quarter = width // 4
    bufs = (xbuf, gbuf, nbuf, xbuf)
    columns = (pl.ds(0, quarter), pl.ds(0, width), pl.ds(0, num_ref.shape[1]), pl.ds(quarter, width - quarter))
    own = (tok_ref.at[:, columns[0]], grad_ref, num_ref, tok_ref.at[:, columns[3]])

    def weight_places(rows):
        return (
            wgu.at[rows, pl.ds(0, hidden)],
            wgu.at[rows, pl.ds(hidden, hidden)],
            wdn.at[rows, :],
        )

    for a in (0, 3, 2, 1):
        for f in range(2):
            start(own[a], bufs[a].at[slot(f, 1), core, :, columns[a]], ring_send.at[a, f, 0], ring_recv.at[a, f, 0], flows[f])
    for k, ref in enumerate((wg_ref, wu_ref, wd_ref)):
        start(ref, weight_places(own_at)[k], w_send.at[k], w_recv.at[k], other)
    for a in (0, 3, 2, 1):
        start(own[a], bufs[a].at[0, core, :, columns[a]], sib_send.at[a, 0], sib_recv.at[a, 0], sibling)
    for buf, ref in ((xbuf, tok_ref), (gbuf, grad_ref), (nbuf, num_ref)):
        buf[0, core] = ref[...]
    wgu[own_at, pl.ds(0, hidden)] = wg_ref[...]
    wgu[own_at, pl.ds(hidden, hidden)] = wu_ref[...]
    wdn[own_at, :] = wd_ref[...]

    def part(a, s, c, step, f):
        if step == half_ring:
            n = bufs[a].shape[2] // 2
            return bufs[a].at[s, c, pl.ds(f * n, n), columns[a]]
        return bufs[a].at[s, c, :, columns[a]]

    def arrive(a, step):
        for f in range(2):
            ref = part(a, slot(f, step), core, step, f)
            copy(ref, ref, ring_send.at[a, f, step - 1], ring_recv.at[a, f, step - 1], flows[f]).wait_recv()
            if step < half_ring:
                src = part(a, slot(f, step), core, step + 1, f)
                dst = part(a, slot(f, step + 1), core, step + 1, f)
                start(src, dst, ring_send.at[a, f, step], ring_recv.at[a, f, step], flows[f])
            k = 2 * step - 1 + f
            start(ref, ref, sib_send.at[a, k], sib_recv.at[a, k], sibling)

    def arrive_sibling(step, arrays=(0, 3, 2, 1)):
        for a in arrays:
            for f in range(2 if step else 1):
                ref = part(a, slot(f, step), 1 - core, step, f)
                k = 2 * step - 1 + f if step else 0
                copy(ref, ref, sib_send.at[a, k], sib_recv.at[a, k], sibling).wait_recv()

    per_slot = 2 * block
    row_ids = lax.broadcasted_iota(jnp.int32, (2 * experts, 256), 0)
    col_ids = lax.broadcasted_iota(jnp.int32, (2 * experts, 256), 1)
    wanted = jnp.where(col_ids < 128, me, experts)
    select = jnp.where(row_ids == wanted, 1.0, 0.0).astype(BF16)

    def span(slots):
        return pl.ds(slots[0] * per_slot, len(slots) * per_slot)

    def tokens_of(slots, cols=slice(None)):
        return xbuf[slots[0] : slots[-1] + 1, :, :, cols].reshape(len(slots) * per_slot, -1)

    def scale(slots):
        for s in slots:
            for b in range(2):
                both = contract_rows(nbuf[s, b], select)
                gate = both[:, :128] / both[:, 128:]
                for k in range(width // 128):
                    cols = pl.ds(k * 128, 128)
                    scaled[pl.ds(s * per_slot + b * block, block), cols] = (
                        gate * gbuf[s, b, :, cols].astype(F32)
                    ).astype(BF16)

    def pre_part(slots, at):
        x = tokens_of(slots, at)
        return jnp.dot(x, wgu[at, :], preferred_element_type=F32)

    def ga_part(slots, at):
        return jnp.dot(scaled[span(slots), at], wdn[at, :], preferred_element_type=F32)

    def pointwise(slots, pre, grad_act):
        where = span(slots)
        pre_gate = pre[:, :hidden]
        pre_up = pre[:, hidden:]
        sig = jax.nn.sigmoid(pre_gate)
        silu = pre_gate * sig
        acts[where, :] = (silu * pre_up).astype(BF16)
        grads[where, pl.ds(hidden, hidden)] = (grad_act * silu).astype(BF16)
        grads[where, pl.ds(0, hidden)] = (
            grad_act * pre_up * sig * (1.0 + pre_gate * (1.0 - sig))
        ).astype(BF16)

    def back(slots):
        rows = lax.dot_general(
            grads[span(slots), :], wgu[...], (((1,), (1,)), ((), ())), preferred_element_type=F32
        )
        cbuf[slots[0] : slots[-1] + 1] = rows.astype(BF16).reshape(len(slots), 2, block, width)
        for s in slots:
            start(cbuf.at[s, 1 - core], sbuf.at[s], row_send.at[s], row_recv.at[s], sibling)

    def terms(slots, at, k):
        where = span(slots)
        if k == 2:
            return contract_rows(scaled[where, at], acts[where, :])
        return contract_rows(tokens_of(slots, at), grads[where, pl.ds(k * hidden, hidden)])

    def wait_weight(k):
        ref = weight_places(other_at)[k]
        copy(ref, ref, w_send.at[k], w_recv.at[k], other).wait_recv()

    half = block // 2
    got_rows = set()

    def row_sum(s, h):
        if s not in got_rows:
            got_rows.add(s)
            copy(sbuf.at[s], sbuf.at[s], row_send.at[s], row_recv.at[s], sibling).wait_recv()
        at = pl.ds(h * half, half)
        return cbuf[s, core, at].astype(F32) + sbuf[s, at].astype(F32)

    def order(f):
        listed = [(half_ring - 1, 1 - f), (half_ring, f), (half_ring - 1, f)]
        for d in range(half_ring - 2, 0, -1):
            listed += [(d, 1 - f), (d, f)]
        return listed

    def incoming(f, d, h):
        j = order(f).index((d + 1, h))
        ref = rbuf.at[f, j]
        copy(ref, ref, sum_send.at[f, j], sum_recv.at[f, j], flows[f]).wait_recv()
        return rbuf[f, j].astype(F32)

    def send_sums(j):
        for f in range(2):
            d, h = order(f)[j]
            value = row_sum(slot(1 - f, d), h)
            if (d + 1, h) in order(f):
                value = value + incoming(f, d, h)
            obuf[f, j] = value.astype(BF16)
            start(obuf.at[f, j], rbuf.at[f, j], sum_send.at[f, j], sum_recv.at[f, j], flows[f])

    slots_a, slots_b, slots_c, slots_d, slots_e = [0], [1, 2], [3, 4], [5, 6], [7]
    everything = slice(None)

    def point(slots):
        pointwise(slots, pre_buf[span(slots), :], ga_buf[span(slots), :])

    arrive_sibling(0)
    scale(slots_a)
    pre_buf[span(slots_a), :] = pre_part(slots_a, own_at)
    ga_buf[span(slots_a), :] = ga_part(slots_a, own_at)
    arrive(0, 1)
    arrive(3, 1)
    arrive_sibling(1, (0, 3))
    pre_buf[span(slots_b), :] = pre_part(slots_b, own_at)
    arrive(2, 1)
    arrive(1, 1)
    arrive_sibling(1, (1, 2))
    scale(slots_b)
    ga_buf[span(slots_b), :] = ga_part(slots_b, own_at)
    arrive(0, 2)
    arrive(3, 2)
    arrive_sibling(2, (0, 3))
    wait_weight(0)
    wait_weight(1)
    pre_buf[span(slots_a), :] += pre_part(slots_a, other_at)
    pre_buf[span(slots_b), :] += pre_part(slots_b, other_at)
    arrive(2, 2)
    arrive(1, 2)
    pre_buf[span(slots_c), :] = pre_part(slots_c, everything)
    arrive_sibling(2, (1, 2))
    scale(slots_c)
    wait_weight(2)
    ga_buf[span(slots_a), :] += ga_part(slots_a, other_at)
    point(slots_a)
    ga_buf[span(slots_b), :] += ga_part(slots_b, other_at)
    point(slots_b)
    arrive(0, 3)
    arrive(3, 3)
    ga_buf[span(slots_c), :] = ga_part(slots_c, everything)
    point(slots_c)
    arrive_sibling(3, (0, 3))
    pre_buf[span(slots_d), :] = pre_part(slots_d, everything)
    arrive(2, 3)
    arrive(1, 3)
    slots_abc = slots_a + slots_b + slots_c
    for k in range(2):
        acc_gu[:, pl.ds(k * hidden, hidden)] = terms(slots_abc, other_at, k)
    acc_d[...] = terms(slots_abc, other_at, 2)
    arrive_sibling(3, (1, 2))
    scale(slots_d)
    ga_buf[span(slots_d), :] = ga_part(slots_d, everything)
    point(slots_d)
    arrive(0, 4)
    arrive(3, 4)
    arrive(2, 4)
    back(slots_d)
    arrive_sibling(4, (0, 3, 2))
    pre_e = pre_part(slots_e, everything)
    pre_buf[span(slots_e), :] = pre_e
    for k in range(2):
        acc_gu[:, pl.ds(k * hidden, hidden)] += terms(slots_d, other_at, k)
    acc_d[...] += terms(slots_d, other_at, 2)
    send_sums(0)
    arrive(1, 4)
    arrive_sibling(4, (1,))
    scale(slots_e)
    ga_buf[span(slots_e), :] = ga_part(slots_e, everything)
    point(slots_e)

    def send_term(k):
        held = acc_d[...] if k == 2 else acc_gu[:, pl.ds(k * hidden, hidden)]
        pbuf[k] = (held + terms(slots_e, other_at, k)).astype(BF16)
        start(pbuf.at[k], qbuf.at[k], part_send.at[k], part_recv.at[k], other)

    send_term(0)
    back(slots_e)
    send_term(1)

    outs = (out_gate, out_up, out_down)

    def own_term(k):
        outs[k][...] = terms(list(range(chips)), own_at, k).astype(BF16)

    between = {
        1: lambda: (send_term(2), back(slots_c)),
        2: lambda: back(slots_b),
        3: lambda: back(slots_a),
        4: lambda: own_term(0),
        5: lambda: own_term(1),
        6: lambda: own_term(2),
    }

    for j in range(1, len(order(0))):
        send_sums(j)
        if j in between:
            between[j]()
    for h in range(2):
        value = row_sum(0, h) + incoming(0, 0, h) + incoming(1, 0, h)
        out_tok[pl.ds(h * half, half), :] = value.astype(BF16)

    for k, out in enumerate(outs):
        copy(qbuf.at[k], qbuf.at[k], part_send.at[k], part_recv.at[k], other).wait_recv()
        out[...] = (out[...].astype(F32) + qbuf[k].astype(F32)).astype(BF16)
    for op in started:
        op.wait_send()


def write_out(*refs):
    ins, outs, held, sems = refs[:4], refs[4:8], refs[8:12], refs[12]
    reads = [pltpu.make_async_copy(ins[k], held[k], sems.at[k]) for k in range(4)]
    writes = [pltpu.make_async_copy(held[k], outs[k], sems.at[4 + k]) for k in range(4)]
    for op in reads:
        op.start()
    for k in range(4):
        reads[k].wait()
        writes[k].start()
    for op in writes:
        op.wait()


def on_device_dense(tokens, grad_out, expert_ids, gate_numer, w_gate, w_up, w_down):
    peers = lax.axis_size("expert")
    chips = peers // 2
    block, width = tokens.shape
    share, hidden = w_gate.shape[1:]
    depth = share * lax.axis_size("dp")
    messages = chips - 1
    rows = peers * block
    early = rows
    dma = pltpu.SemaphoreType.DMA
    vmem = pl.BlockSpec(memory_space=pltpu.VMEM)
    outs = pl.pallas_call(
        functools.partial(layer_kernel, chips),
        out_shape=(jax.ShapeDtypeStruct((block, width), BF16),)
        + (jax.ShapeDtypeStruct((share, hidden), BF16),) * 3,
        in_specs=[vmem] * 7,
        out_specs=(vmem,) * 4,
        scratch_shapes=[
            pltpu.VMEM((chips, 2, block, width), BF16),
            pltpu.VMEM((chips, 2, block, width), BF16),
            pltpu.VMEM((chips, 2, 2 * peers, block), BF16),
            pltpu.VMEM((chips, 2, block, width), BF16),
            pltpu.VMEM((chips, block, width), BF16),
            pltpu.VMEM((2, messages, block // 2, width), BF16),
            pltpu.VMEM((2, messages, block // 2, width), BF16),
            pltpu.VMEM((depth, 2 * hidden), BF16),
            pltpu.VMEM((depth, hidden), BF16),
            pltpu.VMEM((share, 2 * hidden), F32),
            pltpu.VMEM((share, hidden), F32),
            pltpu.VMEM((3, share, hidden), BF16),
            pltpu.VMEM((3, share, hidden), BF16),
            pltpu.VMEM((rows, width), BF16),
            pltpu.VMEM((rows, 2 * hidden), BF16),
            pltpu.VMEM((rows, hidden), BF16),
            pltpu.VMEM((early, 2 * hidden), F32),
            pltpu.VMEM((early, hidden), F32),
            pltpu.VMEM((2 * peers, block), BF16),
            dma((3,)), dma((3,)),
            dma((4, 2, chips // 2)), dma((4, 2, chips // 2)),
            dma((4, chips + 1)), dma((4, chips + 1)),
            dma((chips,)), dma((chips,)),
            dma((2, messages)), dma((2, messages)),
            dma((3,)), dma((3,)),
        ],
        compiler_params=pltpu.CompilerParams(
            collective_id=0, has_side_effects=True, vmem_limit_bytes=58 * 1024 * 1024
        ),
        cost_estimate=pl.CostEstimate(
            flops=16 * peers * block * width * hidden, bytes_accessed=8 * block * width, transcendentals=0
        ),
    )(tokens, grad_out, expert_ids.T, gate_numer.T, w_gate[0], w_up[0], w_down[0])
    outs = pl.pallas_call(
        write_out,
        out_shape=tuple(jax.ShapeDtypeStruct(value.shape, value.dtype) for value in outs),
        in_specs=[pl.BlockSpec(memory_space=pltpu.HBM)] * 4,
        out_specs=(pl.BlockSpec(memory_space=pltpu.HBM),) * 4,
        scratch_shapes=[pltpu.VMEM(value.shape, value.dtype) for value in outs] + [dma((8,))],
    )(*outs)
    return (outs[0],) + tuple(value[None] for value in outs[1:])


def solution(mesh):
    return jax.shard_map(
        on_device_dense if mesh.shape["expert"] == 16 else on_device_routed,
        mesh=mesh,
        in_specs=(
            P(("dp", "expert"), None),
            P(("dp", "expert"), None),
            P(("dp", "expert"), None),
            P(("dp", "expert"), None),
            P("expert", "dp", None),
            P("expert", "dp", None),
            P("expert", "dp", None),
        ),
        out_specs=(
            P(("dp", "expert"), None),
            P("expert", "dp", None),
            P("expert", "dp", None),
            P("expert", "dp", None),
        ),
        check_vma=False,
    )
```

profile of v0, /device:TPU:0, one launch (start us, length us, event | category | flops | bytes accessed | tf_op | source)
XLA Modules:
  0.0 84.0 jit_solution(17063168592129545086)
XLA Ops:
  0.6 81.1 %shard_map.102 = (bf16[128,1024]{1,0:T(8,128)(2,1)}, bf16[512,384]{1,0:T(8,128)(2,1)}, bf16[512,384]{1,0:T(8,128)(2,1)}, bf16[512,384]{1,0:T(8,128)(2,1)}) custom-call(bf16[128,1024]{1,0:T(8,128)(2,1)} %tok_ref.1, bf16[128,1024]{1,0:T(8,128)(2,1)} %grad_ref.1, s32[8,128]{1,0:T(8,128)} %bitcast.14, s32[8,128]{1,0:T(8,128)} %bitcast.15, ...), custom_call_target="tpu_custom_call" | custom-call | flops 12884901888 | bytes 1048576 | tf_op jit(solution)/shard_map/pallas_call | solution.py:453
  81.7 2.2 %shard_map.103 = (bf16[128,1024]{1,0:T(8,128)(2,1)}, bf16[512,384]{1,0:T(8,128)(2,1)}, bf16[512,384]{1,0:T(8,128)(2,1)}, bf16[512,384]{1,0:T(8,128)(2,1)}) custom-call(bf16[128,1024]{1,0:T(8,128)(2,1)} %get-tuple-element.12.refs_0_, bf16[512,384]{1,0:T(8,128)(2,1)} %get-tuple-element.13.refs_1_, bf16[512,384]{1,0:T(8,128)(2,1)} %get-tuple-element.14.refs_2_, ...), custom_call_target="tpu_custom_call" | custom-call | tf_op jit(solution)/shard_map/pallas_call | solution.py:493
where the time goes:
time: 84.2 us; the launch traced here: 84 us
  Pallas kernels  83.2 us (99%)
    pallas_call x1, Pallas kernels, on_device_dense(): pl.pallas_call(functools.partial(layer_kernel, chips), out_shape=(jax.Sha...  81.1 us
    pallas_call x1, Pallas kernels, on_device_dense(): pl.pallas_call(write_out, out_shape=tuple((jax.ShapeDtypeStruct(value.sha...  2.15 us

commit v1 on v0

--- a/solution.py
+++ b/solution.py
@@ -113,7 +113,7 @@
 def layer_kernel(
     chips, tok_ref, grad_ref, ids_ref, numer_ref, wg_ref, wu_ref, wd_ref,
     out_tok, out_gate, out_up, out_down,
-    xbuf, gbuf, nbuf, cbuf, sbuf, obuf, rbuf, wgu, wdn, acc_gu, acc_d, pbuf, qbuf, scaled, grads, acts,
+    xbuf, gbuf, nbuf, cbuf, sbuf, obuf, rbuf, wgu, wdn, acc_gu, pbuf, qbuf, scaled, grads, acts,
     pre_buf, ga_buf, num_ref,
     w_send, w_recv, ring_send, ring_recv, sib_send, sib_recv,
     row_send, row_recv, sum_send, sum_recv, part_send, part_recv,
@@ -179,10 +179,8 @@
     def slot(f, d):
         return 0 if d == 0 else min(2 * d - 1 + f, chips - 1)
 
-    quarter = width // 4
-    bufs = (xbuf, gbuf, nbuf, xbuf)
-    columns = (pl.ds(0, quarter), pl.ds(0, width), pl.ds(0, num_ref.shape[1]), pl.ds(quarter, width - quarter))
-    own = (tok_ref.at[:, columns[0]], grad_ref, num_ref, tok_ref.at[:, columns[3]])
+    bufs = (xbuf, gbuf, nbuf)
+    own = (tok_ref, grad_ref, num_ref)
 
     def weight_places(rows):
         return (
@@ -191,13 +189,17 @@
             wdn.at[rows, :],
         )
 
-    for a in (0, 3, 2, 1):
+    for a in (0, 2, 1):
         for f in range(2):
-            start(own[a], bufs[a].at[slot(f, 1), core, :, columns[a]], ring_send.at[a, f, 0], ring_recv.at[a, f, 0], flows[f])
-    for k, ref in enumerate((wg_ref, wu_ref, wd_ref)):
-        start(ref, weight_places(own_at)[k], w_send.at[k], w_recv.at[k], other)
-    for a in (0, 3, 2, 1):
-        start(own[a], bufs[a].at[0, core, :, columns[a]], sib_send.at[a, 0], sib_recv.at[a, 0], sibling)
+            start(own[a], bufs[a].at[slot(f, 1), core], ring_send.at[a, f, 0], ring_recv.at[a, f, 0], flows[f])
+    weights = [
+        copy(ref, weight_places(own_at)[k], w_send.at[k], w_recv.at[k], other)
+        for k, ref in enumerate((wg_ref, wu_ref, wd_ref))
+    ]
+    for op in weights[:2]:
+        op.start()
+    for a in (0, 2, 1):
+        start(own[a], bufs[a].at[0, core], sib_send.at[a, 0], sib_recv.at[a, 0], sibling)
     for buf, ref in ((xbuf, tok_ref), (gbuf, grad_ref), (nbuf, num_ref)):
         buf[0, core] = ref[...]
     wgu[own_at, pl.ds(0, hidden)] = wg_ref[...]
@@ -207,8 +209,8 @@
     def part(a, s, c, step, f):
         if step == half_ring:
             n = bufs[a].shape[2] // 2
-            return bufs[a].at[s, c, pl.ds(f * n, n), columns[a]]
-        return bufs[a].at[s, c, :, columns[a]]
+            return bufs[a].at[s, c, pl.ds(f * n, n)]
+        return bufs[a].at[s, c]
 
     def arrive(a, step):
         for f in range(2):
@@ -221,7 +223,7 @@
             k = 2 * step - 1 + f
             start(ref, ref, sib_send.at[a, k], sib_recv.at[a, k], sibling)
 
-    def arrive_sibling(step, arrays=(0, 3, 2, 1)):
+    def arrive_sibling(step, arrays=(0, 2, 1)):
         for a in arrays:
             for f in range(2 if step else 1):
                 ref = part(a, slot(f, step), 1 - core, step, f)
@@ -319,6 +321,7 @@
             obuf[f, j] = value.astype(BF16)
             start(obuf.at[f, j], rbuf.at[f, j], sum_send.at[f, j], sum_recv.at[f, j], flows[f])
 
+    slots_abc = [0, 1, 2, 3, 4]
     slots_a, slots_b, slots_c, slots_d, slots_e = [0], [1, 2], [3, 4], [5, 6], [7]
     everything = slice(None)
 
@@ -330,58 +333,53 @@
     pre_buf[span(slots_a), :] = pre_part(slots_a, own_at)
     ga_buf[span(slots_a), :] = ga_part(slots_a, own_at)
     arrive(0, 1)
-    arrive(3, 1)
-    arrive_sibling(1, (0, 3))
+    arrive(2, 1)
+    arrive_sibling(1, (0, 2))
     pre_buf[span(slots_b), :] = pre_part(slots_b, own_at)
-    arrive(2, 1)
     arrive(1, 1)
-    arrive_sibling(1, (1, 2))
+    arrive_sibling(1, (1,))
     scale(slots_b)
     ga_buf[span(slots_b), :] = ga_part(slots_b, own_at)
+    for op in weights[:2]:
+        op.wait_send()
+    weights[2].start()
+    started.append(weights[2])
     arrive(0, 2)
-    arrive(3, 2)
-    arrive_sibling(2, (0, 3))
     wait_weight(0)
     wait_weight(1)
     pre_buf[span(slots_a), :] += pre_part(slots_a, other_at)
     pre_buf[span(slots_b), :] += pre_part(slots_b, other_at)
     arrive(2, 2)
     arrive(1, 2)
+    arrive_sibling(2, (0, 2))
     pre_buf[span(slots_c), :] = pre_part(slots_c, everything)
-    arrive_sibling(2, (1, 2))
+    arrive_sibling(2, (1,))
     scale(slots_c)
     wait_weight(2)
     ga_buf[span(slots_a), :] += ga_part(slots_a, other_at)
     point(slots_a)
+    arrive(0, 3)
+    arrive(2, 3)
     ga_buf[span(slots_b), :] += ga_part(slots_b, other_at)
     point(slots_b)
-    arrive(0, 3)
-    arrive(3, 3)
     ga_buf[span(slots_c), :] = ga_part(slots_c, everything)
     point(slots_c)
-    arrive_sibling(3, (0, 3))
+    arrive_sibling(3, (0, 2))
     pre_buf[span(slots_d), :] = pre_part(slots_d, everything)
-    arrive(2, 3)
     arrive(1, 3)
-    slots_abc = slots_a + slots_b + slots_c
     for k in range(2):
         acc_gu[:, pl.ds(k * hidden, hidden)] = terms(slots_abc, other_at, k)
-    acc_d[...] = terms(slots_abc, other_at, 2)
-    arrive_sibling(3, (1, 2))
+    arrive_sibling(3, (1,))
     scale(slots_d)
     ga_buf[span(slots_d), :] = ga_part(slots_d, everything)
     point(slots_d)
     arrive(0, 4)
-    arrive(3, 4)
     arrive(2, 4)
     back(slots_d)
-    arrive_sibling(4, (0, 3, 2))
-    pre_e = pre_part(slots_e, everything)
-    pre_buf[span(slots_e), :] = pre_e
     for k in range(2):
         acc_gu[:, pl.ds(k * hidden, hidden)] += terms(slots_d, other_at, k)
-    acc_d[...] += terms(slots_d, other_at, 2)
-    send_sums(0)
+    arrive_sibling(4, (0, 2))
+    pre_buf[span(slots_e), :] = pre_part(slots_e, everything)
     arrive(1, 4)
     arrive_sibling(4, (1,))
     scale(slots_e)
@@ -389,11 +387,15 @@
     point(slots_e)
 
     def send_term(k):
-        held = acc_d[...] if k == 2 else acc_gu[:, pl.ds(k * hidden, hidden)]
-        pbuf[k] = (held + terms(slots_e, other_at, k)).astype(BF16)
+        if k == 2:
+            value = terms(list(range(chips)), other_at, k)
+        else:
+            value = acc_gu[:, pl.ds(k * hidden, hidden)] + terms(slots_e, other_at, k)
+        pbuf[k] = value.astype(BF16)
         start(pbuf.at[k], qbuf.at[k], part_send.at[k], part_recv.at[k], other)
 
     send_term(0)
+    send_sums(0)
     back(slots_e)
     send_term(1)
 
@@ -467,7 +469,6 @@
             pltpu.VMEM((depth, 2 * hidden), BF16),
             pltpu.VMEM((depth, hidden), BF16),
             pltpu.VMEM((share, 2 * hidden), F32),
-            pltpu.VMEM((share, hidden), F32),
             pltpu.VMEM((3, share, hidden), BF16),
             pltpu.VMEM((3, share, hidden), BF16),
             pltpu.VMEM((rows, width), BF16),
@@ -477,8 +478,8 @@
             pltpu.VMEM((early, hidden), F32),
             pltpu.VMEM((2 * peers, block), BF16),
             dma((3,)), dma((3,)),
-            dma((4, 2, chips // 2)), dma((4, 2, chips // 2)),
-            dma((4, chips + 1)), dma((4, chips + 1)),
+            dma((3, 2, chips // 2)), dma((3, 2, chips // 2)),
+            dma((3, chips + 1)), dma((3, chips + 1)),
             dma((chips,)), dma((chips,)),
             dma((2, messages)), dma((2, messages)),
             dma((3,)), dma((3,)),

time: 84.2 us -> 83.3 us (0.989)
  Pallas kernels: 83.2 us -> 82.3 us
    pallas_call x1, Pallas kernels: 81.1 us -> 80.1 us  [on_device_dense(): pl.pallas_call(functools.partial(layer_kernel, chips), out_shape=(jax.Sha...]
where the time goes in v1:
time: 83.3 us; the launch traced here: 83.1 us
  Pallas kernels  82.3 us (99%)
    pallas_call x1, Pallas kernels, on_device_dense(): pl.pallas_call(functools.partial(layer_kernel, chips), out_shape=(jax.Sha...  80.1 us
    pallas_call x1, Pallas kernels, on_device_dense(): pl.pallas_call(write_out, out_shape=tuple((jax.ShapeDtypeStruct(value.sha...  2.15 us

profile of v1, /device:TPU:0, one launch (start us, length us, event | category | flops | bytes accessed | tf_op | source)
XLA Modules:
  0.0 83.1 jit_solution(12802160056915747271)
XLA Ops:
  0.6 80.1 %shard_map.102 = (bf16[128,1024]{1,0:T(8,128)(2,1)}, bf16[512,384]{1,0:T(8,128)(2,1)}, bf16[512,384]{1,0:T(8,128)(2,1)}, bf16[512,384]{1,0:T(8,128)(2,1)}) custom-call(bf16[128,1024]{1,0:T(8,128)(2,1)} %tok_ref.1, bf16[128,1024]{1,0:T(8,128)(2,1)} %grad_ref.1, s32[8,128]{1,0:T(8,128)} %bitcast.14, s32[8,128]{1,0:T(8,128)} %bitcast.15, ...), custom_call_target="tpu_custom_call" | custom-call | flops 12884901888 | bytes 1048576 | tf_op jit(solution)/shard_map/pallas_call | solution.py:455
  80.8 2.2 %shard_map.103 = (bf16[128,1024]{1,0:T(8,128)(2,1)}, bf16[512,384]{1,0:T(8,128)(2,1)}, bf16[512,384]{1,0:T(8,128)(2,1)}, bf16[512,384]{1,0:T(8,128)(2,1)}) custom-call(bf16[128,1024]{1,0:T(8,128)(2,1)} %get-tuple-element.12.refs_0_, bf16[512,384]{1,0:T(8,128)(2,1)} %get-tuple-element.13.refs_1_, bf16[512,384]{1,0:T(8,128)(2,1)} %get-tuple-element.14.refs_2_, ...), custom_call_target="tpu_custom_call" | custom-call | tf_op jit(solution)/shard_map/pallas_call | solution.py:494
